TPU v7x, 32 devices: a whole 2x2x4 slice. The times are simulated.
32 devices in a mesh: groups: 2 (over y), dp: 4 (over z), tensor: 2 (over x), section: 2 (over core).
Axes of the slice: x: 2, y: 2, z: 4, core: 2. Of those that a mesh axis runs over, the one named last changes fastest.
Arguments:
- tokens: bfloat16 [512, 8192], P(('groups', 'dp'), 'tensor'), parts along dimension 0, may hold values from -120 to 120
- norm_gain: float32 [8192], P('tensor'), may hold values from 0.25 to 1.75
- gate_weight: bfloat16 [8192, 24576], P('tensor', ('dp', 'section')), may hold values from -0.0625 to 0.0625
- up_weight: bfloat16 [8192, 24576], P('tensor', ('dp', 'section')), may hold values from -0.0625 to 0.0625
- down_weight: bfloat16 [24576, 8192], P(('dp', 'section'), 'tensor'), may hold values from -0.0390625 to 0.0390625
- lengths: int32 [8], P('groups'), parts along dimension 0, may hold values from 1 to 64, 96 in all
Outputs:
- mixed: bfloat16 [512, 8192], P(('groups', 'dp', 'section'), 'tensor'), parts along dimension 0
There are 2 independent parts, one for each index of `groups`. A program takes and returns all parts, laid end to end along the dimension named above; an argument that names none is the same for every part. Nothing has to cross between parts.
Inputs may be any that keep to these rules, and one draw needn't show every extreme that they name: lengths[i] live rows stand at the head of data shard i's 64 slots; the lengths sum to 96 and the largest equals 64.
All inputs are finite; a program needn't handle non-finite values.
Results may differ from a plain program's by a relative error of at most 0.019.
Values may be sent and summed in bfloat16 or wider, within the bound.
A program may use at most 192 MiB of HBM per device.

v0:
```python
import jax
import jax.numpy as jnp
from jax import lax
from jax.sharding import PartitionSpec as P

D = 8192


norm_epsilon = 1e-05


def mix_units(summed, unit_count):
    return (jax.nn.silu(summed[:, :unit_count]) * summed[:, unit_count:]).astype(jnp.bfloat16)


def unit_values(partial_value, unit_count):
    summed = lax.psum(partial_value.astype(jnp.bfloat16), "tensor").astype(jnp.float32)
    result = mix_units(summed, unit_count)
    return result


def per_device(tokens, norm_gain, gate_weight, up_weight, down_weight, lengths):
    slot_count = tokens.shape[0]
    shard_total = lax.axis_size("dp")
    section_total = lax.axis_size("section")
    unit_count = gate_weight.shape[1]
    padded_rows = slot_count * shard_total
    widened = tokens.astype(jnp.float32)
    squares = lax.psum(jnp.sum(widened * widened, axis=1), "tensor")
    scaling = lax.rsqrt(squares / D + norm_epsilon)
    normed = (widened * scaling[:, None] * norm_gain[None, :]).astype(jnp.bfloat16)
    both_weights = jnp.concatenate([gate_weight, up_weight], axis=1)
    shard_starts = jnp.cumsum(lengths) - lengths
    live_total = padded_rows * 3 // 8
    gathered = lax.all_gather(normed, "dp", axis=0, tiled=True)
    position = jnp.arange(live_total, dtype=jnp.int32)
    shard_ends = shard_starts + lengths
    owner_shard = jnp.sum((position[:, None] >= shard_ends[None, :]).astype(jnp.int32), axis=1)
    shard_numbers = jnp.arange(shard_total, dtype=jnp.int32)
    owner_start = jnp.sum(
        jnp.where(owner_shard[:, None] == shard_numbers[None, :], shard_starts[None, :], 0), axis=1
    )
    source_rows = owner_shard * slot_count + position - owner_start
    compact_rows = jnp.take(gathered, source_rows, axis=0)
    partial_value = jnp.dot(compact_rows, both_weights, preferred_element_type=jnp.float32)
    compact_hidden = unit_values(partial_value, unit_count)
    compact_down = jnp.dot(compact_hidden, down_weight, preferred_element_type=jnp.float32)
    half_rows = slot_count // section_total
    padded_index = jnp.arange(lax.axis_size(("dp", "section")) * half_rows, dtype=jnp.int32)
    slot_of = padded_index % slot_count
    shard_of = padded_index // slot_count
    live_slot = slot_of < jnp.take(lengths, shard_of, axis=0)
    target = jnp.clip(jnp.take(shard_starts, shard_of, axis=0) + slot_of, 0, live_total - 1)
    branch = lax.psum_scatter(
        jnp.where(live_slot[:, None], jnp.take(compact_down, target, axis=0), 0.0).astype(
            jnp.bfloat16
        ),
        ("dp", "section"),
        scatter_dimension=0,
        tiled=True,
    ).astype(jnp.float32)
    my_slots = lax.axis_index("section") * half_rows + jnp.arange(half_rows, dtype=jnp.int32)
    own_length = lengths[lax.axis_index("dp")]
    return jnp.where((my_slots < own_length)[:, None], branch, 0.0).astype(jnp.bfloat16)


def solution(mesh):
    in_specs = (
        P(("groups", "dp"), "tensor"),
        P("tensor"),
        P("tensor", ("dp", "section")),
        P("tensor", ("dp", "section")),
        P(("dp", "section"), "tensor"),
        P("groups"),
    )
    out_specs = P(("groups", "dp", "section"), "tensor")
    return jax.shard_map(
        per_device, mesh=mesh, in_specs=in_specs, out_specs=out_specs, check_vma=False
    )
```

profile of v0, /device:TPU:0, one launch (start us, length us, event | category | flops | bytes accessed | tf_op | source)
XLA Modules:
  0.0 188.6 jit_solution(4445780991244365657)
XLA Ops:
  6.5 0.0 all-gather.2.cloned.1.call-start
  6.5 1.2 fusion.8
  7.8 5.8 %psum.14 = f32[64]{0:T(128)S(1)} all-reduce(f32[64]{0:T(128)S(1)} %fusion.8), channel_id=1, replica_groups=mesh['groups'=2,'dp'=4,'tensor'=2,'section'=2] {'tensor'}, use_global_device_ids=true, to_apply=%region_4.6 | all-reduce | flops 64 | bytes 512 | tf_op jit(solution)/shard_map/psum | solution.py:29
  13.6 2.0 %fusion.10 = bf16[64,4096]{1,0:T(8,128)(2,1)} fusion(bf16[64,4096]{1,0:T(8,128)(2,1)} %param.8, f32[4096]{0:T(1024)} %param.9, f32[64]{0:T(128)S(1)} %add_rsqrt_fusion), kind=kLoop, calls=%fused_computation.14 | loop fusion | flops 1048576 | bytes 1065216 | tf_op jit(solution)/shard_map/convert_element_type | solution.py:31
  15.7 0.0 all-gather.2.cloned.1.call-update
  15.7 0.0 all-reduce.2.cloned.1.call-start
  15.7 0.8 reduce-window.8
  16.6 0.1 convert_reduce_fusion
  16.7 0.7 bitcast_subtract_fusion.1
  17.3 0.1 select_reduce_fusion
  17.4 46.2 %all-gather.2.cloned.1.call-done = bf16[256,4096]{1,0:T(8,128)(2,1)} async-done(((bf16[64,4096]{1,0:T(8,128)(2,1)}), bf16[256,4096]{1,0:T(8,128)(2,1)}) %all-gather.2.cloned.1.call-update) | async-done | bytes 2097168 | tf_op jit(solution)/shard_map/all_gather | solution.py:35
  63.6 3.6 %gather_fusion = bf16[96,4096]{1,0:T(8,128)(2,1)S(1)} fusion(bf16[256,4096]{1,0:T(8,128)(2,1)} %all-gather.2.cloned.1.call-done, s32[1024]{0:T(1024)S(1)} %pad_clamp_fusion.1), kind=kCustom, calls=%fused_computation | custom fusion | bytes 1573248 | tf_op jit(solution)/shard_map/jit(_take)/gather | solution.py:44
  67.2 0.0 copy-start
  67.3 19.0 %fusion.4 = bf16[96,6144]{1,0:T(8,128)(2,1)} fusion(bf16[4096,3072]{1,0:T(8,128)(2,1)} %param.11, bf16[4096,3072]{1,0:T(8,128)(2,1)} %param.10, bf16[96,4096]{1,0:T(8,128)(2,1)S(1)} %gather_fusion, pred[96]{0:T(512)(128)(4,1)S(1)} %compare_and_fusion.1), kind=kOutput, calls=%fused_computation.6 | convolution fusion | flops 4933484544 | bytes 52297824 | tf_op jit(solution)/shard_map/dot_general | solution.py:45
  86.2 0.0 all-reduce.2.cloned.1.call-update
  86.3 0.0 reduce-scatter.2.cloned.1.call-start
  86.3 0.0 copy-done
  86.3 0.7 fusion.23
  87.0 2.5 %select_compare_fusion = pred[256]{0:T(512)(128)(4,1)S(1)} fusion(s32[]{:T(128)} %bitcast.4, s32[]{:T(128)} %bitcast.3, s32[]{:T(128)} %bitcast.2, s32[]{:T(128)} %bitcast.1), kind=kLoop, calls=%fused_computation.40 | loop fusion | flops 6656 | bytes 272 | tf_op jit(solution)/shard_map/lt | solution.py:52
  89.5 0.7 fusion.24
  90.2 2.5 %compare_and_fusion.2 = (pred[256]{0:T(512)(128)(4,1)S(1)}, s32[256]{0:T(256)S(1)}) fusion(s32[]{:T(128)} %bitcast.10, s32[]{:T(128)} %bitcast.9, s32[]{:T(128)} %bitcast.8, s32[]{:T(128)} %bitcast.7), kind=kLoop, calls=%fused_computation.33 | loop fusion | flops 8448 | bytes 1296 | tf_op jit(solution)/shard_map/jit(_take)/and | solution.py:55
  92.7 35.3 %all-reduce.2.cloned.1.call-done = bf16[96,6144]{1,0:T(8,128)(2,1)} async-done(((bf16[96,6144]{1,0:T(8,128)(2,1)}), bf16[96,6144]{1,0:T(8,128)(2,1)}) %all-reduce.2.cloned.1.call-update) | async-done | bytes 1179664 | tf_op jit(solution)/shard_map/psum | solution.py:17
  128.1 1.5 convert_element_type.31
  129.5 10.4 %fusion.13 = bf16[96,4096]{1,0:T(8,128)(2,1)S(1)} fusion(bf16[3072,4096]{1,0:T(8,128)(2,1)} %param.12, f32[96,6144]{1,0:T(8,128)S(1)} %convert_element_type.31), kind=kOutput, calls=%fused_computation.17 | convolution fusion | flops 2417688576 | bytes 28311552 | tf_op jit(solution)/shard_map/dot_general | solution.py:47
  139.9 1.8 gather_fusion.1
  141.8 2.5 %select_convert_fusion = bf16[256,4096]{1,0:T(8,128)(2,1)} fusion(bf16[256,4096]{1,0:T(8,128)(2,1)S(1)} %gather_fusion.1, pred[256]{0:T(512)(128)(4,1)S(1)} %get-tuple-element.6, pred[256]{0:T(512)(128)(4,1)S(1)} %select_compare_fusion), kind=kLoop, calls=%fused_computation.7 | loop fusion | flops 2097152 | bytes 4194816 | tf_op jit(solution)/shard_map/convert_element_type | solution.py:55
  144.3 0.0 reduce-scatter.2.cloned.1.call-update
  144.3 0.6 add_compare_fusion
  144.9 35.3 %reduce-scatter.2.cloned.1.call-done = bf16[32,4096]{1,0:T(8,128)(2,1)} async-done(((bf16[256,4096]{1,0:T(8,128)(2,1)}), bf16[32,4096]{1,0:T(8,128)(2,1)}) %reduce-scatter.2.cloned.1.call-update) | async-done | bytes 262160 | tf_op jit(solution)/shard_map/reduce_scatter | solution.py:54
  180.3 1.8 select_convert_fusion.1
  (5 shorter events, 0.0 us)
Async XLA Ops:
  6.5 57.1 %all-gather.2.cloned.1.call-start = ((), (), s32[]{:S(2)}) async-start(), calls=%async_computation.1 | async-start | bytes 2621440 | tf_op jit(solution)/shard_map/all_gather | solution.py:35
  15.7 112.4 %all-reduce.2.cloned.1.call-start = ((), (), s32[]{:S(2)}) async-start(), calls=%async_computation.2 | async-start | bytes 2359296 | tf_op jit(solution)/shard_map/psum | solution.py:17
  67.2 19.1 %copy-start = (s32[4]{0:T(128)S(1)}, s32[4]{0:T(128)}, u32[]{:S(2)}) copy-start(s32[4]{0:T(128)} %param.13) | copy-start | bytes 52
  86.3 94.0 %reduce-scatter.2.cloned.1.call-start = ((), (), s32[]{:S(2)}) async-start(), calls=%async_computation.3 | async-start | bytes 2359296 | tf_op jit(solution)/shard_map/reduce_scatter | solution.py:54
Sparse Core Ops, SparseCore 0:
  15.8 47.7 all-gather.1
  86.4 41.6 all-reduce.1
  144.5 35.7 reduce-scatter.1
where the time goes:
time: 189 us
  waiting for transfers between devices  117 us (62%)
  matrix products  29.4 us (16%)
  other arithmetic  16.3 us (9%)
  between operations  13.2 us (7%)
  local copies, waits for them, and re-layouts  6.84 us (4%)
  blocking collectives  5.84 us (3%)
    all_gather x1, waiting for transfers between devices, per_device(): gathered = lax.all_gather(normed, 'dp', axis=0, tiled=True)  46.2 us
    reduce_scatter x1, waiting for transfers between devices, per_device(): lax.psum_scatter(jnp.where(live_slot[:, None], jnp.take(compact_down, tar...  35.3 us
    psum x1, waiting for transfers between devices, unit_values(): lax.psum(partial_value.astype(jnp.bfloat16), 'tensor').astype(jnp.float32)  35.3 us
    dot_general x1, matrix products, per_device(): jnp.dot(compact_rows, both_weights, preferred_element_type=jnp.float32)  19 us
    dot_general x1, matrix products, per_device(): jnp.dot(compact_hidden, down_weight, preferred_element_type=jnp.float32)  10.4 us
    psum x1, blocking collectives, per_device(): squares = lax.psum(jnp.sum(widened * widened, axis=1), 'tensor')  5.84 us
  transfers between devices with their start and end apart: 3, of which 3 were waited for; matrix products, arithmetic and copies ran while one was open for 5% of the time, Pallas kernels for 0%

commit v1 on v0

v1 whole, which is shorter than its diff:
```python
import functools

import jax
import jax.numpy as jnp
from jax import lax
from jax.experimental import pallas as pl
from jax.experimental.pallas import tpu as pltpu
from jax.sharding import PartitionSpec as P

norm_epsilon = 1e-05
f32, bf16 = jnp.float32, jnp.bfloat16
MESH = pl.DeviceIdType.MESH
LAG = 3


def aligned(value, unit):
    return pl.multiple_of(value, unit)


def kernel(
    size,
    tokens, gain, gate_weight, up_weight, down_weight, lengths, out,
    tok, gate_buf, up_buf, down_buf,
    own, right_out, right_in, left_out, left_in, rows, normed, squares, squares_in,
    part, part_in, hidden,
    partial, sib_out, sib_in, zright_out, zright_in, zleft_out, zleft_in, final_out, out_buf,
    tok_sem, gate_sem, up_sem, down_sem,
    ring_send, ring_recv, rows_send, rows_recv, squares_send, squares_recv,
    part_send, part_recv, hidden_send, hidden_recv,
    sib_send, sib_recv, zring_send, zring_recv, final_send, final_recv, out_sem,
):
    n, nt, live, slots = size["n"], size["nt"], size["live"], size["slots"]
    ka, wa, nc, wu, nb, nj, wj = (size[x] for x in ("ka", "wa", "nc", "wu", "nb", "nj", "wj"))
    width = tokens.shape[1]
    half, hj, hs, rt = width // 2, wj // 2, slots // 2, live // nt
    z, t, s = lax.axis_index("dp"), lax.axis_index("tensor"), lax.axis_index("section")
    peers = [lax.rem(t + i, nt) for i in range(1, nt)]
    sib = {"section": 1 - s}
    far = jnp.maximum(z, n - 1 - z)

    def gate_copy(c):
        slot = lax.rem(c, nb)
        cols = pl.ds(aligned(c * wu, 128), wu)
        return (
            pltpu.make_async_copy(gate_weight.at[:, cols], gate_buf.at[slot], gate_sem.at[slot]),
            pltpu.make_async_copy(up_weight.at[:, cols], up_buf.at[slot], up_sem.at[slot]),
        )

    def down_copy(j):
        return pltpu.make_async_copy(
            down_weight.at[:, pl.ds(aligned(j * wj, 128), wj)], down_buf.at[j], down_sem.at[j]
        )

    def remote(src, dst, send, recv, where):
        return pltpu.make_async_remote_copy(
            src_ref=src, dst_ref=dst, send_sem=send, recv_sem=recv, device_id=where,
            device_id_type=MESH,
        )

    tok_copy = pltpu.make_async_copy(tokens, tok, tok_sem)
    tok_copy.start()

    @pl.loop(0, nb)
    def _(c):
        for copy in gate_copy(c):
            copy.start()

    @pl.loop(0, nj)
    def _(j):
        down_copy(j).start()

    barrier = pltpu.get_barrier_semaphore()
    for p in peers:
        pl.semaphore_signal(barrier, inc=1, device_id={"tensor": p}, device_id_type=MESH)
    pl.semaphore_signal(barrier, inc=1, device_id=sib, device_id_type=MESH)

    @pl.when(z > 0)
    def _():
        pl.semaphore_signal(barrier, inc=1, device_id={"dp": z - 1}, device_id_type=MESH)

    @pl.when(z < n - 1)
    def _():
        pl.semaphore_signal(barrier, inc=1, device_id={"dp": z + 1}, device_id_type=MESH)

    start = jnp.int32(0)
    mine = jnp.int32(0)
    for i in range(n):
        start = start + jnp.where(i < z, lengths[i], 0)
        mine = mine + jnp.where(i == z, lengths[i], 0)

    place_row = lax.broadcasted_iota(jnp.int32, (live, slots), 0)
    place_slot = lax.broadcasted_iota(jnp.int32, (live, slots), 1)
    place = jnp.where(
        (place_row == place_slot + start) & (place_slot < mine), 1.0, 0.0
    ).astype(bf16)

    @pl.when(z == 0)
    def _():
        right_in[...] = jnp.zeros_like(right_in)
        zright_in[...] = jnp.zeros_like(zright_in)

    @pl.when(z == n - 1)
    def _():
        left_in[...] = jnp.zeros_like(left_in)
        zleft_in[...] = jnp.zeros_like(zleft_in)

    tok_copy.wait()
    for k in range(ka):
        cols = pl.ds(aligned(s * half + k * wa, 128), wa)
        own[k] = jnp.dot(place, tok[:, cols], preferred_element_type=f32).astype(bf16)

    pl.semaphore_wait(
        barrier, nt + jnp.where(z > 0, 1, 0) + jnp.where(z < n - 1, 1, 0)
    )

    def right_copy(k):
        return remote(right_out.at[k], right_in.at[k], ring_send.at[0, k], ring_recv.at[0, k],
                      {"dp": jnp.where(z < n - 1, z + 1, z - 1)})

    def left_copy(k):
        return remote(left_out.at[k], left_in.at[k], ring_send.at[1, k], ring_recv.at[1, k],
                      {"dp": jnp.where(z > 0, z - 1, z + 1)})

    def rows_copy(k, side):
        cols = pl.ds(aligned(side * half + k * wa, 128), wa)
        return remote(rows.at[:, cols], rows.at[:, cols], rows_send.at[k], rows_recv.at[k], sib)

    squares[...] = jnp.zeros_like(squares)

    def absorb(k, side):
        cols = pl.ds(aligned(side * half + k * wa, 128), wa)
        wide = rows[:, cols].astype(f32)
        total = squares[...]
        for q in range(wa // 128):
            piece = wide[:, q * 128:(q + 1) * 128]
            total = total + piece * piece
        squares[...] = total
        normed[:, cols] = (wide * gain[:, cols]).astype(bf16)

    @pl.loop(0, ka + n - 1)
    def _(m):
        kr, kl, kx = m - z, m - (n - 1 - z), m - far

        @pl.when((kr >= 0) & (kr < ka))
        def _():
            @pl.when(z > 0)
            def _():
                right_copy(kr).wait_recv()

            @pl.when(z < n - 1)
            def _():
                right_out[kr] = own[kr] + right_in[kr]
                right_copy(kr).start()

        @pl.when((kl >= 0) & (kl < ka))
        def _():
            @pl.when(z < n - 1)
            def _():
                left_copy(kl).wait_recv()

            @pl.when(z > 0)
            def _():
                left_out[kl] = own[kl] + left_in[kl]
                left_copy(kl).start()

        @pl.when((kx >= 0) & (kx < ka))
        def _():
            cols = pl.ds(aligned(s * half + kx * wa, 128), wa)
            rows[:, cols] = own[kx] + right_in[kx] + left_in[kx]
            rows_copy(kx, s).start()
            absorb(kx, s)

    @pl.loop(0, ka)
    def _(k):
        rows_copy(k, 1 - s).wait_recv()
        absorb(k, 1 - s)

    my_rows = pl.ds(aligned(t * rt, 16), rt)

    def rows_of(p):
        return pl.ds(aligned(p * rt, 16), rt)

    def squares_copy(p):
        return remote(squares.at[rows_of(p)], squares_in.at[t], squares_send.at[p],
                      squares_recv.at[t], {"tensor": p})

    def squares_arrival(p):
        return remote(squares.at[rows_of(p)], squares_in.at[p], squares_send.at[p],
                      squares_recv.at[p], {"tensor": p})

    def part_copy(p, c):
        return remote(part.at[c, rows_of(p)], part_in.at[t, c], part_send.at[p, c],
                      part_recv.at[t, c], {"tensor": p})

    def part_arrival(p, c):
        return remote(part.at[c, rows_of(p)], part_in.at[p, c], part_send.at[p, c],
                      part_recv.at[p, c], {"tensor": p})

    def hidden_copy(p, c):
        place_at = hidden.at[my_rows, pl.ds(aligned(c * wu, 128), wu)]
        return remote(place_at, place_at, hidden_send.at[p, c], hidden_recv.at[t, c],
                      {"tensor": p})

    def hidden_arrival(p, c):
        place_at = hidden.at[rows_of(p), pl.ds(aligned(c * wu, 128), wu)]
        return remote(place_at, place_at, hidden_send.at[p, c], hidden_recv.at[p, c],
                      {"tensor": p})

    for p in peers:
        squares_copy(p).start()

    @pl.loop(0, nc + LAG)
    def _(c):
        @pl.when(c < nc)
        def _():
            slot = lax.rem(c, nb)
            for copy in gate_copy(c):
                copy.wait()
            part[c, :, :wu] = jnp.dot(
                normed[...], gate_buf[slot], preferred_element_type=f32
            ).astype(bf16)
            part[c, :, wu:] = jnp.dot(
                normed[...], up_buf[slot], preferred_element_type=f32
            ).astype(bf16)
            for p in peers:
                part_copy(p, c).start()

            @pl.when(c + nb < nc)
            def _():
                for copy in gate_copy(c + nb):
                    copy.start()

        @pl.when(c == LAG)
        def _():
            total = squares[my_rows]
            for p in peers:
                squares_arrival(p).wait_recv()
                total = total + squares_in[p]
            mean = jnp.sum(total, axis=1, keepdims=True) / (width * nt)
            squares_in[t] = jnp.broadcast_to(lax.rsqrt(mean + norm_epsilon), (rt, 128))

        @pl.when(c >= LAG)
        def _():
            done = c - LAG
            both = part[done, my_rows].astype(f32)
            for p in peers:
                part_arrival(p, done).wait_recv()
                both = both + part_in[p, done].astype(f32)
            scaling = squares_in[t][:, :1]
            gate = both[:, :wu] * scaling
            up = both[:, wu:] * scaling
            hidden[my_rows, pl.ds(aligned(done * wu, 128), wu)] = (
                gate / (1.0 + jnp.exp(-gate)) * up
            ).astype(bf16)
            for p in peers:
                hidden_copy(p, done).start()

    @pl.loop(0, nc)
    def _(c):
        for p in peers:
            hidden_arrival(p, c).wait_recv()

    pick_slot = lax.broadcasted_iota(jnp.int32, (slots, live), 0)
    pick_row = lax.broadcasted_iota(jnp.int32, (slots, live), 1)
    pick = jnp.where(
        (pick_row == pick_slot + start) & (pick_slot < mine), 1.0, 0.0
    ).astype(bf16)

    def zright_copy(k):
        return remote(zright_out.at[k], zright_in.at[k], zring_send.at[0, k], zring_recv.at[0, k],
                      {"dp": jnp.where(z < n - 1, z + 1, z - 1)})

    def zleft_copy(k):
        return remote(zleft_out.at[k], zleft_in.at[k], zring_send.at[1, k], zring_recv.at[1, k],
                      {"dp": jnp.where(z > 0, z - 1, z + 1)})

    def sib_copy(k):
        return remote(sib_out.at[k], sib_in.at[k], sib_send.at[k], sib_recv.at[k], sib)

    def final_copy(k, side):
        return remote(final_out.at[k], out_buf.at[:, pl.ds(aligned(k * wj + side * hj, 128), hj)],
                      final_send.at[k], final_recv.at[k], sib)

    @pl.loop(0, nj + n)
    def _(m):
        @pl.when(m < nj)
        def _():
            down_copy(m).wait()
            both = jnp.dot(hidden[...], down_buf[m], preferred_element_type=f32)
            low, high = both[:, :hj], both[:, hj:]
            sib_out[m] = jnp.where(s == 0, high, low).astype(bf16)
            sib_copy(m).start()
            partial[m] = jnp.where(s == 0, low, high)

        k = m - 1

        @pl.when((k >= 0) & (k < nj))
        def _():
            sib_copy(k).wait_recv()
            partial[k] = partial[k] + sib_in[k].astype(f32)

        kr, kl, kx = k - z, k - (n - 1 - z), k - far

        @pl.when((kr >= 0) & (kr < nj))
        def _():
            @pl.when(z > 0)
            def _():
                zright_copy(kr).wait_recv()

            @pl.when(z < n - 1)
            def _():
                zright_out[kr] = (partial[kr] + zright_in[kr].astype(f32)).astype(bf16)
                zright_copy(kr).start()

        @pl.when((kl >= 0) & (kl < nj))
        def _():
            @pl.when(z < n - 1)
            def _():
                zleft_copy(kl).wait_recv()

            @pl.when(z > 0)
            def _():
                zleft_out[kl] = (partial[kl] + zleft_in[kl].astype(f32)).astype(bf16)
                zleft_copy(kl).start()

        @pl.when((kx >= 0) & (kx < nj))
        def _():
            total = partial[kx] + zright_in[kx].astype(f32) + zleft_in[kx].astype(f32)
            picked = jnp.dot(pick, total.astype(bf16), preferred_element_type=f32)
            low, high = picked[:hs], picked[hs:]
            final_out[kx] = jnp.where(s == 0, high, low).astype(bf16)
            final_copy(kx, s).start()
            out_buf[:, pl.ds(aligned(kx * wj + s * hj, 128), hj)] = jnp.where(
                s == 0, low, high
            ).astype(bf16)

    @pl.loop(0, nj)
    def _(k):
        final_copy(k, 1 - s).wait_recv()

    out_copy = pltpu.make_async_copy(out_buf, out, out_sem)
    out_copy.start()

    @pl.loop(0, ka)
    def _(k):
        rows_copy(k, s).wait_send()

        @pl.when(z < n - 1)
        def _():
            right_copy(k).wait_send()

        @pl.when(z > 0)
        def _():
            left_copy(k).wait_send()

    for p in peers:
        squares_copy(p).wait_send()

    @pl.loop(0, nc)
    def _(c):
        for p in peers:
            part_copy(p, c).wait_send()
            hidden_copy(p, c).wait_send()

    @pl.loop(0, nj)
    def _(k):
        sib_copy(k).wait_send()
        final_copy(k, s).wait_send()

        @pl.when(z < n - 1)
        def _():
            zright_copy(k).wait_send()

        @pl.when(z > 0)
        def _():
            zleft_copy(k).wait_send()

    out_copy.wait()


def per_device(tokens, norm_gain, gate_weight, up_weight, down_weight, lengths):
    n, nt = lax.axis_size("dp"), lax.axis_size("tensor")
    slots, width = tokens.shape
    units = gate_weight.shape[1]
    live = slots * n * 3 // 8
    rt = live // nt
    ka = 4
    wa = width // 2 // ka
    wu = 256
    nc = units // wu
    nb = min(5, nc)
    wj = 512
    nj = width // wj
    hj, hs = wj // 2, slots // 2
    size = dict(n=n, nt=nt, live=live, slots=slots, ka=ka, wa=wa, nc=nc, wu=wu, nb=nb, nj=nj, wj=wj)
    V, S = pltpu.VMEM, pltpu.SemaphoreType.DMA
    anywhere = pl.BlockSpec(memory_space=pl.ANY)
    return pl.pallas_call(
        functools.partial(kernel, size),
        out_shape=jax.ShapeDtypeStruct((hs, width), bf16),
        in_specs=[
            anywhere,
            pl.BlockSpec(memory_space=pltpu.VMEM),
            anywhere,
            anywhere,
            anywhere,
            pl.BlockSpec(memory_space=pltpu.SMEM),
        ],
        out_specs=anywhere,
        scratch_shapes=[
            V((slots, width), bf16),
            V((nb, width, wu), bf16),
            V((nb, width, wu), bf16),
            V((nj, units, wj), bf16),
            V((ka, live, wa), bf16),
            V((ka, live, wa), bf16),
            V((ka, live, wa), bf16),
            V((ka, live, wa), bf16),
            V((ka, live, wa), bf16),
            V((live, width), bf16),
            V((live, width), bf16),
            V((live, 128), f32),
            V((nt, rt, 128), f32),
            V((nc, live, 2 * wu), bf16),
            V((nt, nc, rt, 2 * wu), bf16),
            V((live, units), bf16),
            V((nj, live, hj), f32),
            V((nj, live, hj), bf16),
            V((nj, live, hj), bf16),
            V((nj, live, hj), bf16),
            V((nj, live, hj), bf16),
            V((nj, live, hj), bf16),
            V((nj, live, hj), bf16),
            V((nj, hs, hj), bf16),
            V((hs, width), bf16),
            S, S((nb,)), S((nb,)), S((nj,)),
            S((2, ka)), S((2, ka)), S((ka,)), S((ka,)), S((nt,)), S((nt,)),
            S((nt, nc)), S((nt, nc)), S((nt, nc)), S((nt, nc)),
            S((nj,)), S((nj,)), S((2, nj)), S((2, nj)), S((nj,)), S((nj,)), S,
        ],
        compiler_params=pltpu.CompilerParams(
            collective_id=0, has_side_effects=True, vmem_limit_bytes=63 * 2**20
        ),
        cost_estimate=pl.CostEstimate(
            flops=6 * live * width * units,
            bytes_accessed=6 * width * units,
            transcendentals=live * units,
        ),
    )(tokens, norm_gain.reshape(1, width), gate_weight, up_weight, down_weight, lengths)


def solution(mesh):
    in_specs = (
        P(("groups", "dp"), "tensor"),
        P("tensor"),
        P("tensor", ("dp", "section")),
        P("tensor", ("dp", "section")),
        P(("dp", "section"), "tensor"),
        P("groups"),
    )
    out_specs = P(("groups", "dp", "section"), "tensor")
    return jax.shard_map(
        per_device, mesh=mesh, in_specs=in_specs, out_specs=out_specs, check_vma=False
    )
```

time: 189 us -> 85 us (0.45)
  waiting for transfers between devices: 117 us -> 0 us
  Pallas kernels: 0 us -> 82.5 us
  matrix products: 29.4 us -> 0 us
  other arithmetic: 16.3 us -> 0 us
  between operations: 13.2 us -> 0.01 us
  blocking collectives: 5.84 us -> 0 us
  local copies, waits for them, and re-layouts: 6.84 us -> 1.67 us
    pallas_call x0 -> x1, Pallas kernels: none -> 82.5 us  [per_device(): pl.pallas_call(functools.partial(kernel, size), out_shape=jax.ShapeDtypeS...]
    all_gather x1 -> x0, waiting for transfers between devices: 46.2 us -> none  [per_device(): gathered = lax.all_gather(normed, 'dp', axis=0, tiled=True)]
    reduce_scatter x1 -> x0, waiting for transfers between devices: 35.3 us -> none  [per_device(): lax.psum_scatter(jnp.where(live_slot[:, None], jnp.take(compact_down, tar...]
    psum x1 -> x0, waiting for transfers between devices: 35.3 us -> none  [unit_values(): lax.psum(partial_value.astype(jnp.bfloat16), 'tensor').astype(jnp.float32)]
    dot_general x2 -> x0, matrix products: 29.4 us -> none  [the longest x1 19 us: per_device(): jnp.dot(compact_rows, both_weights, preferred_element_type=jnp.float32)]
    convert_element_type x4 -> x0, other arithmetic: 7.78 us -> none  [the longest x1 2.5 us: per_device(): jnp.where(live_slot[:, None], jnp.take(compact_down, target, axis=0), 0.0)]
    gather x3 -> x0, local copies, waits for them, and re-layouts: 6.16 us -> none  [the longest x1 3.65 us: per_device(): compact_rows = jnp.take(gathered, source_rows, axis=0)]
    psum x1 -> x0, blocking collectives: 5.84 us -> none  [per_device(): squares = lax.psum(jnp.sum(widened * widened, axis=1), 'tensor')]
  transfers between devices with their start and end apart: 3 -> 0, of which waited for: 3 -> 0; matrix products, arithmetic and copies ran while one was open for 5% -> 0% of each run, Pallas kernels for 0% -> 0%
where the time goes in v1:
time: 85 us; the launch traced here: 84.2 us
  Pallas kernels  82.5 us (97%)
  local copies, waits for them, and re-layouts  1.67 us (2%)
    pallas_call x1, Pallas kernels, per_device(): pl.pallas_call(functools.partial(kernel, size), out_shape=jax.ShapeDtypeS...  82.5 us

profile of v1, /device:TPU:0, one launch (start us, length us, event | category | flops | bytes accessed | tf_op | source)
XLA Modules:
  0.0 84.2 jit_solution(2195029990946963847)
XLA Ops:
  0.0 82.5 %shard_map.64 = bf16[32,4096]{1,0:T(8,128)(2,1)} custom-call(bf16[64,4096]{1,0:T(8,128)(2,1)} %tokens.1, f32[1,4096]{1,0:T(1,128)} %bitcast.1, bf16[4096,3072]{1,0:T(8,128)(2,1)} %gate_weight.1, bf16[4096,3072]{1,0:T(8,128)(2,1)} %up_weight.1, bf16[3072,4096]{1,0:T(8,128)(2,1)} %down_weight.1, s32[4]{0:T(128)} %lengths.1), custom_call_target="tpu_custom_call" | custom-call | flops 7247757312 | bytes 75497472 | tf_op jit(solution)/shard_map/pallas_call | solution.py:398
  82.6 1.7 %copy.8 = bf16[32,4096]{1,0:T(8,128)(2,1)} copy(bf16[32,4096]{1,0:T(8,128)(2,1)} %shard_map.64) | data formatting | bytes 524288

commit v2 on v1

--- a/solution.py
+++ b/solution.py
@@ -10,7 +10,9 @@
 norm_epsilon = 1e-05
 f32, bf16 = jnp.float32, jnp.bfloat16
 MESH = pl.DeviceIdType.MESH
-LAG = 3
+LAG = 5
+HOP = 3
+SIB = 2
 
 
 def aligned(value, unit):
@@ -137,9 +139,9 @@
         squares[...] = total
         normed[:, cols] = (wide * gain[:, cols]).astype(bf16)
 
-    @pl.loop(0, ka + n - 1)
+    @pl.loop(0, ka + HOP * (n - 1))
     def _(m):
-        kr, kl, kx = m - z, m - (n - 1 - z), m - far
+        kr, kl, kx = m - HOP * z, m - HOP * (n - 1 - z), m - HOP * far
 
         @pl.when((kr >= 0) & (kr < ka))
         def _():
@@ -281,7 +283,7 @@
         return remote(final_out.at[k], out_buf.at[:, pl.ds(aligned(k * wj + side * hj, 128), hj)],
                       final_send.at[k], final_recv.at[k], sib)
 
-    @pl.loop(0, nj + n)
+    @pl.loop(0, nj + SIB + HOP * (n - 1))
     def _(m):
         @pl.when(m < nj)
         def _():
@@ -292,14 +294,14 @@
             sib_copy(m).start()
             partial[m] = jnp.where(s == 0, low, high)
 
-        k = m - 1
+        k = m - SIB
 
         @pl.when((k >= 0) & (k < nj))
         def _():
             sib_copy(k).wait_recv()
             partial[k] = partial[k] + sib_in[k].astype(f32)
 
-        kr, kl, kx = k - z, k - (n - 1 - z), k - far
+        kr, kl, kx = k - HOP * z, k - HOP * (n - 1 - z), k - HOP * far
 
         @pl.when((kr >= 0) & (kr < nj))
         def _():
@@ -384,7 +386,7 @@
     units = gate_weight.shape[1]
     live = slots * n * 3 // 8
     rt = live // nt
-    ka = 4
+    ka = min(8, width // 256)
     wa = width // 2 // ka
     wu = 256
     nc = units // wu

time: 85 us -> 69.4 us (0.82)
  Pallas kernels: 82.5 us -> 66.9 us
    pallas_call x1, Pallas kernels: 82.5 us -> 66.9 us  [per_device(): pl.pallas_call(functools.partial(kernel, size), out_shape=jax.ShapeDtypeS...]
where the time goes in v2:
time: 69.4 us; the launch traced here: 68.6 us
  Pallas kernels  66.9 us (96%)
  local copies, waits for them, and re-layouts  1.67 us (2%)
    pallas_call x1, Pallas kernels, per_device(): pl.pallas_call(functools.partial(kernel, size), out_shape=jax.ShapeDtypeS...  66.9 us
    unnamed x1, local copies, waits for them, and re-layouts  1.67 us

profile of v2, /device:TPU:0, one launch (start us, length us, event | category | flops | bytes accessed | tf_op | source)
XLA Modules:
  0.0 68.6 jit_solution(4104786489917201536)
XLA Ops:
  0.0 66.9 %shard_map.64 = bf16[32,4096]{1,0:T(8,128)(2,1)} custom-call(bf16[64,4096]{1,0:T(8,128)(2,1)} %tokens.1, f32[1,4096]{1,0:T(1,128)} %bitcast.1, bf16[4096,3072]{1,0:T(8,128)(2,1)} %gate_weight.1, bf16[4096,3072]{1,0:T(8,128)(2,1)} %up_weight.1, bf16[3072,4096]{1,0:T(8,128)(2,1)} %down_weight.1, s32[4]{0:T(128)} %lengths.1), custom_call_target="tpu_custom_call" | custom-call | flops 7247757312 | bytes 75497472 | tf_op jit(solution)/shard_map/pallas_call | solution.py:400
  66.9 1.7 %copy.8 = bf16[32,4096]{1,0:T(8,128)(2,1)} copy(bf16[32,4096]{1,0:T(8,128)(2,1)} %shard_map.64) | data formatting | bytes 524288

commit v3 on v2

--- a/solution.py
+++ b/solution.py
@@ -10,9 +10,10 @@
 norm_epsilon = 1e-05
 f32, bf16 = jnp.float32, jnp.bfloat16
 MESH = pl.DeviceIdType.MESH
-LAG = 5
-HOP = 3
-SIB = 2
+LAG = 8
+HOP_ROWS = 4
+HOP_SUMS = 3
+SIB = 1
 
 
 def aligned(value, unit):
@@ -21,12 +22,12 @@
 
 def kernel(
     size,
-    tokens, gain, gate_weight, up_weight, down_weight, lengths, out,
-    tok, gate_buf, up_buf, down_buf,
+    tokens, gain_in, gate_weight, up_weight, down_weight, lengths, out,
+    tok, gain, gate_buf, up_buf, down_buf,
     own, right_out, right_in, left_out, left_in, rows, normed, squares, squares_in,
     part, part_in, hidden,
     partial, sib_out, sib_in, zright_out, zright_in, zleft_out, zleft_in, final_out, out_buf,
-    tok_sem, gate_sem, up_sem, down_sem,
+    tok_sem, gain_sem, gate_sem, up_sem, down_sem,
     ring_send, ring_recv, rows_send, rows_recv, squares_send, squares_recv,
     part_send, part_recv, hidden_send, hidden_recv,
     sib_send, sib_recv, zring_send, zring_recv, final_send, final_recv, out_sem,
@@ -61,6 +62,8 @@
 
     tok_copy = pltpu.make_async_copy(tokens, tok, tok_sem)
     tok_copy.start()
+    gain_copy = pltpu.make_async_copy(gain_in, gain, gain_sem)
+    gain_copy.start()
 
     @pl.loop(0, nb)
     def _(c):
@@ -107,6 +110,7 @@
         zleft_in[...] = jnp.zeros_like(zleft_in)
 
     tok_copy.wait()
+    gain_copy.wait()
     for k in range(ka):
         cols = pl.ds(aligned(s * half + k * wa, 128), wa)
         own[k] = jnp.dot(place, tok[:, cols], preferred_element_type=f32).astype(bf16)
@@ -139,9 +143,9 @@
         squares[...] = total
         normed[:, cols] = (wide * gain[:, cols]).astype(bf16)
 
-    @pl.loop(0, ka + HOP * (n - 1))
+    @pl.loop(0, ka + HOP_ROWS * (n - 1))
     def _(m):
-        kr, kl, kx = m - HOP * z, m - HOP * (n - 1 - z), m - HOP * far
+        kr, kl, kx = m - HOP_ROWS * z, m - HOP_ROWS * (n - 1 - z), m - HOP_ROWS * far
 
         @pl.when((kr >= 0) & (kr < ka))
         def _():
@@ -283,7 +287,7 @@
         return remote(final_out.at[k], out_buf.at[:, pl.ds(aligned(k * wj + side * hj, 128), hj)],
                       final_send.at[k], final_recv.at[k], sib)
 
-    @pl.loop(0, nj + SIB + HOP * (n - 1))
+    @pl.loop(0, nj + SIB + HOP_SUMS * (n - 1))
     def _(m):
         @pl.when(m < nj)
         def _():
@@ -301,7 +305,7 @@
             sib_copy(k).wait_recv()
             partial[k] = partial[k] + sib_in[k].astype(f32)
 
-        kr, kl, kx = k - HOP * z, k - HOP * (n - 1 - z), k - HOP * far
+        kr, kl, kx = k - HOP_SUMS * z, k - HOP_SUMS * (n - 1 - z), k - HOP_SUMS * far
 
         @pl.when((kr >= 0) & (kr < nj))
         def _():
@@ -402,7 +406,7 @@
         out_shape=jax.ShapeDtypeStruct((hs, width), bf16),
         in_specs=[
             anywhere,
-            pl.BlockSpec(memory_space=pltpu.VMEM),
+            anywhere,
             anywhere,
             anywhere,
             anywhere,
@@ -411,6 +415,7 @@
         out_specs=anywhere,
         scratch_shapes=[
             V((slots, width), bf16),
+            V((1, width), f32),
             V((nb, width, wu), bf16),
             V((nb, width, wu), bf16),
             V((nj, units, wj), bf16),
@@ -435,7 +440,7 @@
             V((nj, live, hj), bf16),
             V((nj, hs, hj), bf16),
             V((hs, width), bf16),
-            S, S((nb,)), S((nb,)), S((nj,)),
+            S, S, S((nb,)), S((nb,)), S((nj,)),
             S((2, ka)), S((2, ka)), S((ka,)), S((ka,)), S((nt,)), S((nt,)),
             S((nt, nc)), S((nt, nc)), S((nt, nc)), S((nt, nc)),
             S((nj,)), S((nj,)), S((2, nj)), S((2, nj)), S((nj,)), S((nj,)), S,

time: 69.4 us -> 68.9 us (level)
  no operation moved by 1% of the time
where the time goes in v3:
time: 68.9 us; the launch traced here: 68.2 us
  Pallas kernels  66.5 us (97%)
  local copies, waits for them, and re-layouts  1.67 us (2%)
    pallas_call x1, Pallas kernels, per_device(): pl.pallas_call(functools.partial(kernel, size), out_shape=jax.ShapeDtypeS...  66.5 us
    unnamed x1, local copies, waits for them, and re-layouts  1.67 us

profile of v3, /device:TPU:0, one launch (start us, length us, event | category | flops | bytes accessed | tf_op | source)
XLA Modules:
  0.0 68.2 jit_solution(6592190414168489312)
XLA Ops:
  0.0 66.5 %shard_map.64 = bf16[32,4096]{1,0:T(8,128)(2,1)} custom-call(bf16[64,4096]{1,0:T(8,128)(2,1)} %tokens.1, f32[1,4096]{1,0:T(1,128)} %bitcast.1, bf16[4096,3072]{1,0:T(8,128)(2,1)} %gate_weight.1, bf16[4096,3072]{1,0:T(8,128)(2,1)} %up_weight.1, bf16[3072,4096]{1,0:T(8,128)(2,1)} %down_weight.1, s32[4]{0:T(128)} %lengths.1), custom_call_target="tpu_custom_call" | custom-call | flops 7247757312 | bytes 75497472 | tf_op jit(solution)/shard_map/pallas_call | solution.py:404
  66.5 1.7 %copy.8 = bf16[32,4096]{1,0:T(8,128)(2,1)} copy(bf16[32,4096]{1,0:T(8,128)(2,1)} %shard_map.64) | data formatting | bytes 524288
